TPU v7x, 256 devices: a whole 4x4x8 slice. The times are simulated.
256 devices in a mesh: ctx: 32 (over z, y), head: 8 (over x, core).
Axes of the slice: x: 4, y: 4, z: 8, core: 2. Of those that a mesh axis runs over, the one named last changes fastest.
Arguments:
- token_queries: bfloat16 [8192, 8192], P(('ctx', 'head')), may hold values from -4.5 to 4.5
- token_keys: bfloat16 [8192, 1024], P(('ctx', 'head')), may hold values from -4.5 to 4.5
- token_values: bfloat16 [8192, 1024], P(('ctx', 'head')), may hold values from -6 to 6
- doc_lengths: int32 [16], replicated, may hold values from 1 to 4096, 8192 in all
Outputs:
- attended: bfloat16 [8192, 8192], P(('ctx', 'head'))
Inputs may be any that keep to these rules, and one draw needn't show every extreme that they name: `doc_lengths`: the lengths sum to 8192; the longest is exactly 4096.
All inputs are finite; a program needn't handle non-finite values.
Results may differ from a plain program's by a relative error of at most 0.0035.
Values may be sent and summed in bfloat16 or wider, within the bound.
A program may use at most 64 MiB of HBM per device.

v0:
```python
import functools

import jax
import jax.numpy as jnp
from jax import lax
from jax.experimental import pallas as pl
from jax.experimental.pallas import tpu as pltpu
from jax.sharding import PartitionSpec as P

QUERY_HEADS = 64
KEY_VALUE_HEADS = 8
HEAD_SIZE = 128
DOCS = 16
ROWS = 32
SUPER = 512
HALF = 256
SLOTS = 9
HEADS = 4
WIDE = HEADS * HEAD_SIZE
SCALE2 = HEAD_SIZE ** (-0.5) * 1.4426950408889634
NEGATIVE = -1e30
MESH = pl.DeviceIdType.MESH


def kernel(q_ref, k_ref, v_ref, doc_ref, o_ref, qbuf, kbuf, vbuf, kdoc, qdoc, acc, top, obuf,
           kv_send, kv_recv, q_send, q_recv, z_send, z_recv, y_send, y_recv, s_send, s_recv, o_send, o_recv):
    ctx, head = lax.axis_index("ctx"), lax.axis_index("head")
    z, y = ctx // 4, ctx % 4
    core = head % 2
    yp, yl = y // 2, y % 2
    after, before = lax.rem(z + 1, 8) * 4 + y, lax.rem(z + 7, 8) * 4 + y
    across = z * 4 + 3 - y
    other = head + 1 - 2 * core
    here = z * 8 + head + yl * 256
    me = yl * 8 + head

    def member(i):
        return z * 4 + 2 * yp + i // 8, i % 8

    def heads_of(i):
        parity = (i // 8 + yp) % 2
        group = 2 * ((i % 8) // 2) + parity
        return group, group * 8 + (i % 2) * HEADS

    barrier = pltpu.get_barrier_semaphore()

    def greet(i, _):
        to = lax.rem(me + i, 16)
        c, h = member(to)
        pl.semaphore_signal(barrier, inc=1, device_id=(c, h), device_id_type=MESH)
        return 0

    lax.fori_loop(1, 16, greet, 0)
    for c in (after, before, across):
        pl.semaphore_signal(barrier, inc=1, device_id=(c, head), device_id_type=MESH)
    pl.semaphore_wait(barrier, 18)

    def remote(src, dst, send, recv, to):
        return pltpu.make_async_remote_copy(src_ref=src, dst_ref=dst, send_sem=send, recv_sem=recv,
                                            device_id=to, device_id_type=MESH)

    my_rows = pl.multiple_of(me * ROWS, ROWS)

    def kv_target(j):
        return (j * 2 + yl)

    def kv_copy(j, part, start):
        to = kv_target(j)
        group, _ = heads_of(to)
        ref, buf = ((k_ref, kbuf), (v_ref, vbuf))[part]
        src = ref.at[:, pl.ds(pl.multiple_of(group * HEAD_SIZE, HEAD_SIZE), HEAD_SIZE)]
        dst = buf.at[pl.ds(my_rows, ROWS), :]

        @pl.when(to != me)
        def _():
            copy = remote(src, dst, kv_send.at[part, j], kv_recv.at[part, head], member(to))
            if start:
                copy.start()
            else:
                copy.wait_send()

        if start:
            @pl.when(to == me)
            def _():
                pltpu.make_async_copy(src, dst, kv_recv.at[part, head]).start()

    def kv_arrive(j, part):
        buf = (kbuf, vbuf)[part]
        rows = pl.ds(pl.multiple_of((core * 8 + j) * ROWS, ROWS), ROWS)
        pltpu.make_async_copy(buf.at[rows, :], buf.at[rows, :], kv_recv.at[part, j]).wait()

    def q_copy(i, start):
        to = lax.rem(me + i, 16)
        _, first = heads_of(to)
        src = q_ref.at[:, pl.ds(pl.multiple_of(first * HEAD_SIZE, WIDE), WIDE)]
        dst = qbuf.at[pl.ds(my_rows, ROWS), :]
        copy = remote(src, dst, q_send.at[to], q_recv.at[me], member(to))
        if start:
            copy.start()
        else:
            copy.wait_send()

    def q_own():
        _, first = heads_of(me)
        src = q_ref.at[:, pl.ds(pl.multiple_of(first * HEAD_SIZE, WIDE), WIDE)]
        return pltpu.make_async_copy(src, qbuf.at[pl.ds(my_rows, ROWS), :], q_recv.at[me])

    def q_arrive(i):
        rows = pl.ds(pl.multiple_of(i * ROWS, ROWS), ROWS)
        pltpu.make_async_copy(qbuf.at[rows, :], qbuf.at[rows, :], q_recv.at[i]).wait()

    def loop(n, f, first=0):
        def body(i, _):
            f(i)
            return 0
        lax.fori_loop(first, n, body, 0)

    def piece(buf, slot, half):
        return buf.at[pl.ds(pl.multiple_of(slot * SUPER + half * HALF, HALF), HALF), :]

    def z_copy(d, part):
        buf = (kbuf, vbuf)[part]
        return remote(piece(buf, 2 * d, core), piece(buf, 2 * d + 2, core), z_send.at[part, d],
                      z_recv.at[part, d + 1], (after, head))

    def y_copy(i, part):
        buf = (kbuf, vbuf)[part]
        return remote(piece(buf, 2 * (i + yp), core), piece(buf, 2 * i + 1, core), y_send.at[part, i],
                      y_recv.at[part, i], (across, head))

    def s_copy(slot, part):
        buf = (kbuf, vbuf)[part]
        return remote(piece(buf, slot, core), piece(buf, slot, core), s_send.at[part, slot],
                      s_recv.at[part, slot], (ctx, other))

    def landed(slot, half, sem, part):
        buf = (kbuf, vbuf)[part]
        ref = piece(buf, slot, half)
        pltpu.make_async_copy(ref, ref, sem).wait()

    def pass_on(d):
        for part in (0, 1):
            if d > 0:
                landed(2 * d, core, z_recv.at[part, d], part)
            if d < 4:
                z_copy(d, part).start()

            @pl.when((d - yp >= 0) & (d - yp < 4))
            def _():
                y_copy(jnp.clip(d - yp, 0, 3), part).start()

            s_copy(2 * d, part).start()

    def pass_odd(i):
        for part in (0, 1):
            landed(2 * i + 1, core, y_recv.at[part, i], part)
            s_copy(2 * i + 1, part).start()

    def whole(slot):
        for part in (0, 1):
            landed(slot, 1 - core, s_recv.at[part, slot], part)

    def o_copy(g, i):
        to = lax.rem(me + i, 16)
        _, first = heads_of(me)
        src = obuf.at[g, pl.ds(pl.multiple_of(to * ROWS, ROWS), ROWS), :]
        dst = o_ref.at[:, pl.ds(pl.multiple_of((first + g) * HEAD_SIZE, HEAD_SIZE), HEAD_SIZE)]
        return remote(src, dst, o_send.at[g, to], o_recv.at[g, me], member(to))

    def o_own(g):
        _, first = heads_of(me)
        src = obuf.at[g, pl.ds(my_rows, ROWS), :]
        dst = o_ref.at[:, pl.ds(pl.multiple_of((first + g) * HEAD_SIZE, HEAD_SIZE), HEAD_SIZE)]
        return pltpu.make_async_copy(src, dst, o_recv.at[g, me])

    def o_arrive(g, i):
        _, first = heads_of(i)
        dst = o_ref.at[:, pl.ds(pl.multiple_of((first + g) * HEAD_SIZE, HEAD_SIZE), HEAD_SIZE)]
        pltpu.make_async_copy(dst, dst, o_recv.at[g, i]).wait()

    for part in (0, 1):
        loop(8, lambda j: kv_copy(j, part, True))
    q_own().start()
    loop(16, lambda i: q_copy(i, True), 1)

    lane = lax.broadcasted_iota(jnp.int32, (1, HEAD_SIZE), 1)
    begins = jnp.where(lane == DOCS, -(1 << 20), 1 << 20)
    ends = jnp.where(lane == DOCS, 0, 1 << 20)
    total = jnp.int32(0)
    for j in range(DOCS):
        begins = jnp.where(lane == j, total, begins)
        total = total + doc_ref[j]
        ends = jnp.where(lane == j, total, ends)
    base = (z * 2 + yp) * SUPER

    def one_hot(first, count):
        position = first + lax.broadcasted_iota(jnp.int32, (count, HEAD_SIZE), 0)
        return (position >= begins) & (position < ends)

    qdoc[...] = jnp.where(one_hot(base, SUPER), 0.0, NEGATIVE).astype(jnp.bfloat16)

    def key_documents(slot):
        kdoc[pl.ds(pl.multiple_of(slot * SUPER, SUPER), SUPER), :] = jnp.where(
            one_hot(base - slot * SUPER, SUPER), 1.0, 0.0).astype(jnp.bfloat16)

    loop(SLOTS, key_documents)

    def attend(g, first_slot, slots, kind):
        keys = slots * SUPER
        rows = pl.ds(first_slot * SUPER, keys)
        q = jnp.concatenate([qbuf[:, pl.ds(pl.multiple_of(g * HEAD_SIZE, HEAD_SIZE), HEAD_SIZE)], qdoc[...]], axis=1)
        k = jnp.concatenate([kbuf[rows, :], kdoc[rows, :]], axis=1)
        v = jnp.concatenate([vbuf[rows, :], jnp.ones((keys, HEAD_SIZE), jnp.bfloat16)], axis=1)
        s = lax.dot_general(q, k, (((1,), (1,)), ((), ())), preferred_element_type=jnp.float32)
        if kind != "middle":
            t = lax.broadcasted_iota(jnp.int32, (SUPER, keys), 0)
            u = lax.broadcasted_iota(jnp.int32, (SUPER, keys), 1)
            if kind == "first":
                s = jnp.where(u <= t, s, NEGATIVE)
            else:
                s = jnp.where(u > t + (keys - SUPER), s, NEGATIVE) if slots == 1 else jnp.where(
                    (u < SUPER) | (u - SUPER > t), s, NEGATIVE)
        high = jnp.max(s, axis=1, keepdims=True)
        if kind != "first":
            old = top[g][:, :1]
            high = jnp.maximum(high, old)
        p = jnp.exp2(s * SCALE2 - high * SCALE2).astype(jnp.bfloat16)
        part = jnp.dot(p, v, preferred_element_type=jnp.float32)
        if kind != "first":
            part = part + acc[g] * jnp.exp2((old - high) * SCALE2)
        if kind == "last":
            obuf[g] = (part[:, :HEAD_SIZE] / part[:, HEAD_SIZE:]).astype(jnp.bfloat16)
        else:
            acc[g] = part
            top[g] = jnp.broadcast_to(high, (SUPER, HEAD_SIZE))

    def pair(n, first_slot, slots, kind):
        for g in (2 * n, 2 * n + 1):
            attend(g, first_slot, slots, kind)

    for part in (0, 1):
        loop(8, lambda j: kv_arrive(j, part))
    pass_on(0)
    loop(16, q_arrive)
    whole(0)
    pair(0, 0, 1, "first")
    pass_on(1)
    pair(1, 0, 1, "first")
    pass_odd(0)
    for i in range(1, 5):
        whole(2 * i)
        whole(2 * i - 1)
        kind = "last" if i == 4 else "middle"
        pair(0, 2 * i - 1, 2, kind)
        if i < 4:
            pass_on(i + 1)
        else:
            for g in (0, 1):
                o_own(g).start()
                loop(16, lambda j: o_copy(g, j).start(), 1)
        pair(1, 2 * i - 1, 2, kind)
        if i < 4:
            pass_odd(i)
    for g in (2, 3):
        o_own(g).start()
        loop(16, lambda j: o_copy(g, j).start(), 1)

    for part in (0, 1):
        loop(8, lambda j: kv_copy(j, part, False))
        for d in range(4):
            z_copy(d, part).wait_send()
            y_copy(d, part).wait_send()
        for slot in range(SLOTS):
            s_copy(slot, part).wait_send()
    loop(16, lambda i: q_copy(i, False), 1)
    for g in range(HEADS):
        loop(16, lambda j: o_copy(g, j).wait_send(), 1)
        loop(16, lambda i: o_arrive(g, i))


def on_device(token_queries, token_keys, token_values, doc_lengths):
    dma = pltpu.SemaphoreType.DMA
    any_space = pl.BlockSpec(memory_space=pl.ANY)
    return pl.pallas_call(
        kernel,
        name="packed_attention",
        out_shape=jax.ShapeDtypeStruct((ROWS, QUERY_HEADS * HEAD_SIZE), jnp.bfloat16),
        in_specs=[any_space] * 3 + [pl.BlockSpec(memory_space=pltpu.SMEM)],
        out_specs=any_space,
        scratch_shapes=[
            pltpu.VMEM((SUPER, WIDE), jnp.bfloat16),
            pltpu.VMEM((SLOTS * SUPER, HEAD_SIZE), jnp.bfloat16),
            pltpu.VMEM((SLOTS * SUPER, HEAD_SIZE), jnp.bfloat16),
            pltpu.VMEM((SLOTS * SUPER, HEAD_SIZE), jnp.bfloat16),
            pltpu.VMEM((SUPER, HEAD_SIZE), jnp.bfloat16),
            pltpu.VMEM((HEADS, SUPER, 2 * HEAD_SIZE), jnp.float32),
            pltpu.VMEM((HEADS, SUPER, HEAD_SIZE), jnp.float32),
            pltpu.VMEM((HEADS, SUPER, HEAD_SIZE), jnp.bfloat16),
            dma((2, 8)), dma((2, 8)), dma((16,)), dma((16,)),
            dma((2, 4)), dma((2, 5)), dma((2, 4)), dma((2, 4)),
            dma((2, SLOTS)), dma((2, SLOTS)), dma((HEADS, 16)), dma((HEADS, 16)),
        ],
        compiler_params=pltpu.CompilerParams(
            collective_id=0, has_side_effects=True, vmem_limit_bytes=52 * 2**20),
    )(token_queries, token_keys, token_values, doc_lengths)


def solution(mesh):
    in_specs = (P(("ctx", "head"), None), P(("ctx", "head"), None), P(("ctx", "head"), None), P())
    return jax.shard_map(
        on_device, mesh=mesh, in_specs=in_specs, out_specs=P(("ctx", "head"), None), check_vma=False
    )
```

profile of v0, /device:TPU:1, one launch (start us, length us, event | category | flops | bytes accessed | tf_op | source)
XLA Modules:
  0.0 62.5 jit_solution(10992915040938889394)
XLA Ops:
  0.0 0.0 copy-start
  0.0 1.0 %copy-done = bf16[32,8192]{1,0:T(8,128)(2,1)S(1)} copy-done((bf16[32,8192]{1,0:T(8,128)(2,1)S(1)}, bf16[32,8192]{1,0:T(8,128)(2,1)}, u32[]{:S(2)}) %copy-start) | copy-done | bytes 524312
  1.0 0.0 copy-start.1
  1.0 0.8 %copy-done.1 = bf16[32,1024]{1,0:T(8,128)(2,1)S(1)} copy-done((bf16[32,1024]{1,0:T(8,128)(2,1)S(1)}, bf16[32,1024]{1,0:T(8,128)(2,1)}, u32[]{:S(2)}) %copy-start.1) | copy-done | bytes 65560
  1.9 0.0 copy-start.2
  1.9 0.8 %copy-done.2 = bf16[32,1024]{1,0:T(8,128)(2,1)S(1)} copy-done((bf16[32,1024]{1,0:T(8,128)(2,1)S(1)}, bf16[32,1024]{1,0:T(8,128)(2,1)}, u32[]{:S(2)}) %copy-start.2) | copy-done | bytes 65560
  2.7 0.0 copy-start.3
  2.7 0.7 %copy-done.3 = s32[16]{0:T(128)S(1)} copy-done((s32[16]{0:T(128)S(1)}, s32[16]{0:T(128)}, u32[]{:S(2)}) %copy-start.3) | copy-done | bytes 88
  3.4 58.3 %packed_attention.1 = bf16[32,8192]{1,0:T(8,128)(2,1)S(1)} custom-call(bf16[32,8192]{1,0:T(8,128)(2,1)S(1)} %copy-done, bf16[32,1024]{1,0:T(8,128)(2,1)S(1)} %copy-done.1, bf16[32,1024]{1,0:T(8,128)(2,1)S(1)} %copy-done.2, s32[16]{0:T(128)S(1)} %copy-done.3), custom_call_target="tpu_custom_call" | custom-call | tf_op jit(solution)/shard_map/packed_attention/pallas_call | solution.py:284
  61.7 0.8 %copy.6 = bf16[32,8192]{1,0:T(8,128)(2,1)} copy(bf16[32,8192]{1,0:T(8,128)(2,1)S(1)} %packed_attention.1) | data formatting | bytes 1048576
Async XLA Ops:
  0.0 1.0 %copy-start = (bf16[32,8192]{1,0:T(8,128)(2,1)S(1)}, bf16[32,8192]{1,0:T(8,128)(2,1)}, u32[]{:S(2)}) copy-start(bf16[32,8192]{1,0:T(8,128)(2,1)} %q_ref.1) | copy-start | bytes 1572868
  1.0 0.8 %copy-start.1 = (bf16[32,1024]{1,0:T(8,128)(2,1)S(1)}, bf16[32,1024]{1,0:T(8,128)(2,1)}, u32[]{:S(2)}) copy-start(bf16[32,1024]{1,0:T(8,128)(2,1)} %k_ref.1) | copy-start | bytes 196612
  1.9 0.8 %copy-start.2 = (bf16[32,1024]{1,0:T(8,128)(2,1)S(1)}, bf16[32,1024]{1,0:T(8,128)(2,1)}, u32[]{:S(2)}) copy-start(bf16[32,1024]{1,0:T(8,128)(2,1)} %v_ref.1) | copy-start | bytes 196612
  2.7 0.7 %copy-start.3 = (s32[16]{0:T(128)S(1)}, s32[16]{0:T(128)}, u32[]{:S(2)}) copy-start(s32[16]{0:T(128)} %doc_ref.1) | copy-start | bytes 196
where the time goes:
time: 62.7 us; the launch traced here: 62.5 us
  Pallas kernels  58.3 us (93%)
  local copies, waits for them, and re-layouts  4.17 us (7%)
    pallas_call x1, Pallas kernels, on_device(): pl.pallas_call(kernel, name='packed_attention', out_shape=jax.ShapeDtypeS...  58.3 us
    unnamed x9, local copies, waits for them, and re-layouts  4.17 us

commit v1 on v0

--- a/solution.py
+++ b/solution.py
@@ -16,7 +16,6 @@
 HALF = 256
 SLOTS = 9
 HEADS = 4
-WIDE = HEADS * HEAD_SIZE
 SCALE2 = HEAD_SIZE ** (-0.5) * 1.4426950408889634
 NEGATIVE = -1e30
 MESH = pl.DeviceIdType.MESH
@@ -31,7 +30,6 @@
     after, before = lax.rem(z + 1, 8) * 4 + y, lax.rem(z + 7, 8) * 4 + y
     across = z * 4 + 3 - y
     other = head + 1 - 2 * core
-    here = z * 8 + head + yl * 256
     me = yl * 8 + head
 
     def member(i):
@@ -89,25 +87,25 @@
         rows = pl.ds(pl.multiple_of((core * 8 + j) * ROWS, ROWS), ROWS)
         pltpu.make_async_copy(buf.at[rows, :], buf.at[rows, :], kv_recv.at[part, j]).wait()
 
-    def q_copy(i, start):
+    def q_copy(n, i, start):
         to = lax.rem(me + i, 16)
         _, first = heads_of(to)
-        src = q_ref.at[:, pl.ds(pl.multiple_of(first * HEAD_SIZE, WIDE), WIDE)]
-        dst = qbuf.at[pl.ds(my_rows, ROWS), :]
-        copy = remote(src, dst, q_send.at[to], q_recv.at[me], member(to))
+        src = q_ref.at[:, pl.ds(pl.multiple_of((first + 2 * n) * HEAD_SIZE, 2 * HEAD_SIZE), 2 * HEAD_SIZE)]
+        dst = qbuf.at[n, pl.ds(my_rows, ROWS), :]
+        copy = remote(src, dst, q_send.at[n, to], q_recv.at[n, me], member(to))
         if start:
             copy.start()
         else:
             copy.wait_send()
 
-    def q_own():
+    def q_own(n):
         _, first = heads_of(me)
-        src = q_ref.at[:, pl.ds(pl.multiple_of(first * HEAD_SIZE, WIDE), WIDE)]
-        return pltpu.make_async_copy(src, qbuf.at[pl.ds(my_rows, ROWS), :], q_recv.at[me])
-
-    def q_arrive(i):
+        src = q_ref.at[:, pl.ds(pl.multiple_of((first + 2 * n) * HEAD_SIZE, 2 * HEAD_SIZE), 2 * HEAD_SIZE)]
+        return pltpu.make_async_copy(src, qbuf.at[n, pl.ds(my_rows, ROWS), :], q_recv.at[n, me])
+
+    def q_arrive(n, i):
         rows = pl.ds(pl.multiple_of(i * ROWS, ROWS), ROWS)
-        pltpu.make_async_copy(qbuf.at[rows, :], qbuf.at[rows, :], q_recv.at[i]).wait()
+        pltpu.make_async_copy(qbuf.at[n, rows, :], qbuf.at[n, rows, :], q_recv.at[n, i]).wait()
 
     def loop(n, f, first=0):
         def body(i, _):
@@ -160,28 +158,33 @@
         for part in (0, 1):
             landed(slot, 1 - core, s_recv.at[part, slot], part)
 
-    def o_copy(g, i):
+    def o_copy(n, i):
         to = lax.rem(me + i, 16)
         _, first = heads_of(me)
-        src = obuf.at[g, pl.ds(pl.multiple_of(to * ROWS, ROWS), ROWS), :]
-        dst = o_ref.at[:, pl.ds(pl.multiple_of((first + g) * HEAD_SIZE, HEAD_SIZE), HEAD_SIZE)]
-        return remote(src, dst, o_send.at[g, to], o_recv.at[g, me], member(to))
-
-    def o_own(g):
+        src = obuf.at[n, pl.ds(pl.multiple_of(to * ROWS, ROWS), ROWS), :]
+        dst = o_ref.at[:, pl.ds(pl.multiple_of((first + 2 * n) * HEAD_SIZE, 2 * HEAD_SIZE), 2 * HEAD_SIZE)]
+        return remote(src, dst, o_send.at[n, to], o_recv.at[n, me], member(to))
+
+    def o_own(n):
         _, first = heads_of(me)
-        src = obuf.at[g, pl.ds(my_rows, ROWS), :]
-        dst = o_ref.at[:, pl.ds(pl.multiple_of((first + g) * HEAD_SIZE, HEAD_SIZE), HEAD_SIZE)]
-        return pltpu.make_async_copy(src, dst, o_recv.at[g, me])
-
-    def o_arrive(g, i):
+        src = obuf.at[n, pl.ds(my_rows, ROWS), :]
+        dst = o_ref.at[:, pl.ds(pl.multiple_of((first + 2 * n) * HEAD_SIZE, 2 * HEAD_SIZE), 2 * HEAD_SIZE)]
+        return pltpu.make_async_copy(src, dst, o_recv.at[n, me])
+
+    def o_arrive(n, i):
         _, first = heads_of(i)
-        dst = o_ref.at[:, pl.ds(pl.multiple_of((first + g) * HEAD_SIZE, HEAD_SIZE), HEAD_SIZE)]
-        pltpu.make_async_copy(dst, dst, o_recv.at[g, i]).wait()
+        dst = o_ref.at[:, pl.ds(pl.multiple_of((first + 2 * n) * HEAD_SIZE, 2 * HEAD_SIZE), 2 * HEAD_SIZE)]
+        pltpu.make_async_copy(dst, dst, o_recv.at[n, i]).wait()
+
+    def o_send_pair(n):
+        o_own(n).start()
+        loop(16, lambda j: o_copy(n, j).start(), 1)
 
     for part in (0, 1):
         loop(8, lambda j: kv_copy(j, part, True))
-    q_own().start()
-    loop(16, lambda i: q_copy(i, True), 1)
+    for n in (0, 1):
+        q_own(n).start()
+        loop(16, lambda i: q_copy(n, i, True), 1)
 
     lane = lax.broadcasted_iota(jnp.int32, (1, HEAD_SIZE), 1)
     begins = jnp.where(lane == DOCS, -(1 << 20), 1 << 20)
@@ -208,7 +211,7 @@
     def attend(g, first_slot, slots, kind):
         keys = slots * SUPER
         rows = pl.ds(first_slot * SUPER, keys)
-        q = jnp.concatenate([qbuf[:, pl.ds(pl.multiple_of(g * HEAD_SIZE, HEAD_SIZE), HEAD_SIZE)], qdoc[...]], axis=1)
+        q = jnp.concatenate([qbuf[g // 2, :, (g % 2) * HEAD_SIZE : (g % 2 + 1) * HEAD_SIZE], qdoc[...]], axis=1)
         k = jnp.concatenate([kbuf[rows, :], kdoc[rows, :]], axis=1)
         v = jnp.concatenate([vbuf[rows, :], jnp.ones((keys, HEAD_SIZE), jnp.bfloat16)], axis=1)
         s = lax.dot_general(q, k, (((1,), (1,)), ((), ())), preferred_element_type=jnp.float32)
@@ -229,7 +232,7 @@
         if kind != "first":
             part = part + acc[g] * jnp.exp2((old - high) * SCALE2)
         if kind == "last":
-            obuf[g] = (part[:, :HEAD_SIZE] / part[:, HEAD_SIZE:]).astype(jnp.bfloat16)
+            obuf[g // 2, :, (g % 2) * HEAD_SIZE : (g % 2 + 1) * HEAD_SIZE] = (part[:, :HEAD_SIZE] / part[:, HEAD_SIZE:]).astype(jnp.bfloat16)
         else:
             acc[g] = part
             top[g] = jnp.broadcast_to(high, (SUPER, HEAD_SIZE))
@@ -241,29 +244,27 @@
     for part in (0, 1):
         loop(8, lambda j: kv_arrive(j, part))
     pass_on(0)
-    loop(16, q_arrive)
     whole(0)
+    pass_on(1)
+    loop(16, lambda i: q_arrive(0, i))
     pair(0, 0, 1, "first")
-    pass_on(1)
+    loop(16, lambda i: q_arrive(1, i))
     pair(1, 0, 1, "first")
+    pass_on(2)
     pass_odd(0)
     for i in range(1, 5):
         whole(2 * i)
         whole(2 * i - 1)
         kind = "last" if i == 4 else "middle"
         pair(0, 2 * i - 1, 2, kind)
-        if i < 4:
-            pass_on(i + 1)
-        else:
-            for g in (0, 1):
-                o_own(g).start()
-                loop(16, lambda j: o_copy(g, j).start(), 1)
-        pair(1, 2 * i - 1, 2, kind)
+        if i < 3:
+            pass_on(i + 2)
         if i < 4:
             pass_odd(i)
-    for g in (2, 3):
-        o_own(g).start()
-        loop(16, lambda j: o_copy(g, j).start(), 1)
+        else:
+            o_send_pair(0)
+        pair(1, 2 * i - 1, 2, kind)
+    o_send_pair(1)
 
     for part in (0, 1):
         loop(8, lambda j: kv_copy(j, part, False))
@@ -272,10 +273,11 @@
             y_copy(d, part).wait_send()
         for slot in range(SLOTS):
             s_copy(slot, part).wait_send()
-    loop(16, lambda i: q_copy(i, False), 1)
-    for g in range(HEADS):
-        loop(16, lambda j: o_copy(g, j).wait_send(), 1)
-        loop(16, lambda i: o_arrive(g, i))
+    for n in (0, 1):
+        loop(16, lambda i: q_copy(n, i, False), 1)
+    for n in (0, 1):
+        loop(16, lambda j: o_copy(n, j).wait_send(), 1)
+        loop(16, lambda i: o_arrive(n, i))
 
 
 def on_device(token_queries, token_keys, token_values, doc_lengths):
@@ -288,20 +290,20 @@
         in_specs=[any_space] * 3 + [pl.BlockSpec(memory_space=pltpu.SMEM)],
         out_specs=any_space,
         scratch_shapes=[
-            pltpu.VMEM((SUPER, WIDE), jnp.bfloat16),
+            pltpu.VMEM((2, SUPER, 2 * HEAD_SIZE), jnp.bfloat16),
             pltpu.VMEM((SLOTS * SUPER, HEAD_SIZE), jnp.bfloat16),
             pltpu.VMEM((SLOTS * SUPER, HEAD_SIZE), jnp.bfloat16),
             pltpu.VMEM((SLOTS * SUPER, HEAD_SIZE), jnp.bfloat16),
             pltpu.VMEM((SUPER, HEAD_SIZE), jnp.bfloat16),
             pltpu.VMEM((HEADS, SUPER, 2 * HEAD_SIZE), jnp.float32),
             pltpu.VMEM((HEADS, SUPER, HEAD_SIZE), jnp.float32),
-            pltpu.VMEM((HEADS, SUPER, HEAD_SIZE), jnp.bfloat16),
-            dma((2, 8)), dma((2, 8)), dma((16,)), dma((16,)),
+            pltpu.VMEM((2, SUPER, 2 * HEAD_SIZE), jnp.bfloat16),
+            dma((2, 8)), dma((2, 8)), dma((2, 16)), dma((2, 16)),
             dma((2, 4)), dma((2, 5)), dma((2, 4)), dma((2, 4)),
-            dma((2, SLOTS)), dma((2, SLOTS)), dma((HEADS, 16)), dma((HEADS, 16)),
+            dma((2, SLOTS)), dma((2, SLOTS)), dma((2, 16)), dma((2, 16)),
         ],
         compiler_params=pltpu.CompilerParams(
-            collective_id=0, has_side_effects=True, vmem_limit_bytes=52 * 2**20),
+            collective_id=0, has_side_effects=True, vmem_limit_bytes=63 * 2**20),
     )(token_queries, token_keys, token_values, doc_lengths)
 
 

time: 62.7 us -> 55.3 us (0.88)
  Pallas kernels: 58.3 us -> 53.3 us
  local copies, waits for them, and re-layouts: 4.17 us -> 1.87 us
    pallas_call x1, Pallas kernels: 58.3 us -> 53.3 us  [on_device(): pl.pallas_call(kernel, name='packed_attention', out_shape=jax.ShapeDtypeS...]
    unnamed x9 -> x1, local copies, waits for them, and re-layouts: 4.17 us -> 1.87 us
where the time goes in v1:
time: 55.3 us; the launch traced here: 55.1 us
  Pallas kernels  53.3 us (96%)
  local copies, waits for them, and re-layouts  1.87 us (3%)
    pallas_call x1, Pallas kernels, on_device(): pl.pallas_call(kernel, name='packed_attention', out_shape=jax.ShapeDtypeS...  53.3 us
    unnamed x1, local copies, waits for them, and re-layouts  1.87 us

profile of v1, /device:TPU:1, one launch (start us, length us, event | category | flops | bytes accessed | tf_op | source)
XLA Modules:
  0.0 55.1 jit_solution(16744528595131371389)
XLA Ops:
  0.0 53.3 %packed_attention.1 = bf16[32,8192]{1,0:T(8,128)(2,1)} custom-call(bf16[32,8192]{1,0:T(8,128)(2,1)} %q_ref.1, bf16[32,1024]{1,0:T(8,128)(2,1)} %k_ref.1, bf16[32,1024]{1,0:T(8,128)(2,1)} %v_ref.1, s32[16]{0:T(128)} %doc_ref.1), custom_call_target="tpu_custom_call" | custom-call | tf_op jit(solution)/shard_map/packed_attention/pallas_call | solution.py:286
  53.3 1.9 %copy.6 = bf16[32,8192]{1,0:T(8,128)(2,1)} copy(bf16[32,8192]{1,0:T(8,128)(2,1)} %packed_attention.1) | data formatting | bytes 1048576

commit v2 on v1

--- a/solution.py
+++ b/solution.py
@@ -14,6 +14,7 @@
 ROWS = 32
 SUPER = 512
 HALF = 256
+LEVELS = 8
 SLOTS = 9
 HEADS = 4
 SCALE2 = HEAD_SIZE ** (-0.5) * 1.4426950408889634
@@ -22,12 +23,12 @@
 
 
 def kernel(q_ref, k_ref, v_ref, doc_ref, o_ref, qbuf, kbuf, vbuf, kdoc, qdoc, acc, top, obuf,
-           kv_send, kv_recv, q_send, q_recv, z_send, z_recv, y_send, y_recv, s_send, s_recv, o_send, o_recv):
+           kv_send, kv_recv, q_send, q_recv, z_send, z_recv, y_send, y_recv, s_send, s_recv, o_send, o_recv, q_in, k_in, v_in, in_sem):
     ctx, head = lax.axis_index("ctx"), lax.axis_index("head")
     z, y = ctx // 4, ctx % 4
     core = head % 2
     yp, yl = y // 2, y % 2
-    after, before = lax.rem(z + 1, 8) * 4 + y, lax.rem(z + 7, 8) * 4 + y
+    after, before = jnp.minimum(z + 1, LEVELS - 1) * 4 + y, jnp.maximum(z - 1, 0) * 4 + y
     across = z * 4 + 3 - y
     other = head + 1 - 2 * core
     me = yl * 8 + head
@@ -39,6 +40,11 @@
         parity = (i // 8 + yp) % 2
         group = 2 * ((i % 8) // 2) + parity
         return group, group * 8 + (i % 2) * HEADS
+
+    fetch = [pltpu.make_async_copy(src, dst, in_sem.at[i])
+             for i, (src, dst) in enumerate(((k_ref, k_in), (v_ref, v_in), (q_ref, q_in)))]
+    for copy in fetch:
+        copy.start()
 
     barrier = pltpu.get_barrier_semaphore()
 
@@ -49,9 +55,20 @@
         return 0
 
     lax.fori_loop(1, 16, greet, 0)
-    for c in (after, before, across):
-        pl.semaphore_signal(barrier, inc=1, device_id=(c, head), device_id_type=MESH)
-    pl.semaphore_wait(barrier, 18)
+    pl.semaphore_signal(barrier, inc=1, device_id=(across, head), device_id_type=MESH)
+
+    @pl.when(z < LEVELS - 1)
+    def _():
+        pl.semaphore_signal(barrier, inc=1, device_id=(after, head), device_id_type=MESH)
+
+    @pl.when(z > 0)
+    def _():
+        pl.semaphore_signal(barrier, inc=1, device_id=(before, head), device_id_type=MESH)
+
+    pl.semaphore_wait(barrier, 18 - (z == 0).astype(jnp.int32) - (z == LEVELS - 1).astype(jnp.int32))
+
+    for copy in fetch:
+        copy.wait()
 
     def remote(src, dst, send, recv, to):
         return pltpu.make_async_remote_copy(src_ref=src, dst_ref=dst, send_sem=send, recv_sem=recv,
@@ -65,7 +82,7 @@
     def kv_copy(j, part, start):
         to = kv_target(j)
         group, _ = heads_of(to)
-        ref, buf = ((k_ref, kbuf), (v_ref, vbuf))[part]
+        ref, buf = ((k_in, kbuf), (v_in, vbuf))[part]
         src = ref.at[:, pl.ds(pl.multiple_of(group * HEAD_SIZE, HEAD_SIZE), HEAD_SIZE)]
         dst = buf.at[pl.ds(my_rows, ROWS), :]
 
@@ -90,7 +107,7 @@
     def q_copy(n, i, start):
         to = lax.rem(me + i, 16)
         _, first = heads_of(to)
-        src = q_ref.at[:, pl.ds(pl.multiple_of((first + 2 * n) * HEAD_SIZE, 2 * HEAD_SIZE), 2 * HEAD_SIZE)]
+        src = q_in.at[:, pl.ds(pl.multiple_of((first + 2 * n) * HEAD_SIZE, 2 * HEAD_SIZE), 2 * HEAD_SIZE)]
         dst = qbuf.at[n, pl.ds(my_rows, ROWS), :]
         copy = remote(src, dst, q_send.at[n, to], q_recv.at[n, me], member(to))
         if start:
@@ -100,7 +117,7 @@
 
     def q_own(n):
         _, first = heads_of(me)
-        src = q_ref.at[:, pl.ds(pl.multiple_of((first + 2 * n) * HEAD_SIZE, 2 * HEAD_SIZE), 2 * HEAD_SIZE)]
+        src = q_in.at[:, pl.ds(pl.multiple_of((first + 2 * n) * HEAD_SIZE, 2 * HEAD_SIZE), 2 * HEAD_SIZE)]
         return pltpu.make_async_copy(src, qbuf.at[n, pl.ds(my_rows, ROWS), :], q_recv.at[n, me])
 
     def q_arrive(n, i):
@@ -136,27 +153,48 @@
         ref = piece(buf, slot, half)
         pltpu.make_async_copy(ref, ref, sem).wait()
 
-    def pass_on(d):
-        for part in (0, 1):
-            if d > 0:
-                landed(2 * d, core, z_recv.at[part, d], part)
-            if d < 4:
-                z_copy(d, part).start()
-
-            @pl.when((d - yp >= 0) & (d - yp < 4))
-            def _():
-                y_copy(jnp.clip(d - yp, 0, 3), part).start()
-
-            s_copy(2 * d, part).start()
+    def back_copy(n):
+        if n == 0:
+            return remote(piece(kbuf, 0, core), around, b_send.at[0], b_recv.at[0], (back, head))
+        return remote(around, piece(kbuf, 8, core), b_send.at[1], z_recv.at[0, 4], (back, head))
+
+    def exists(slot):
+        return 2 * z + yp >= slot
+
+    def pass_on(d, parts=(0, 1)):
+        @pl.when(exists(2 * d))
+        def _():
+            for part in parts:
+                if d > 0:
+                    landed(2 * d, core, z_recv.at[part, d], part)
+                if d < 4:
+                    @pl.when(z < LEVELS - 1)
+                    def _():
+                        z_copy(d, part).start()
+                if d == 0:
+                    @pl.when(yp == 0)
+                    def _():
+                        y_copy(0, part).start()
+                elif d == 4:
+                    @pl.when(yp == 1)
+                    def _():
+                        y_copy(3, part).start()
+                else:
+                    y_copy(d - yp, part).start()
+                s_copy(2 * d, part).start()
 
     def pass_odd(i):
-        for part in (0, 1):
-            landed(2 * i + 1, core, y_recv.at[part, i], part)
-            s_copy(2 * i + 1, part).start()
+        @pl.when(exists(2 * i + 1))
+        def _():
+            for part in (0, 1):
+                landed(2 * i + 1, core, y_recv.at[part, i], part)
+                s_copy(2 * i + 1, part).start()
 
     def whole(slot):
-        for part in (0, 1):
-            landed(slot, 1 - core, s_recv.at[part, slot], part)
+        @pl.when(exists(slot))
+        def _():
+            for part in (0, 1):
+                landed(slot, 1 - core, s_recv.at[part, slot], part)
 
     def o_copy(n, i):
         to = lax.rem(me + i, 16)
@@ -207,72 +245,111 @@
             one_hot(base - slot * SUPER, SUPER), 1.0, 0.0).astype(jnp.bfloat16)
 
     loop(SLOTS, key_documents)
-
-    def attend(g, first_slot, slots, kind):
-        keys = slots * SUPER
-        rows = pl.ds(first_slot * SUPER, keys)
-        q = jnp.concatenate([qbuf[g // 2, :, (g % 2) * HEAD_SIZE : (g % 2 + 1) * HEAD_SIZE], qdoc[...]], axis=1)
-        k = jnp.concatenate([kbuf[rows, :], kdoc[rows, :]], axis=1)
-        v = jnp.concatenate([vbuf[rows, :], jnp.ones((keys, HEAD_SIZE), jnp.bfloat16)], axis=1)
+    for slot in range(1, SLOTS):
+        @pl.when(jnp.logical_not(exists(slot)))
+        def _():
+            for buf in (kbuf, vbuf):
+                buf[pl.ds(slot * SUPER, SUPER), :] = jnp.zeros((SUPER, HEAD_SIZE), jnp.bfloat16)
+
+    def attend(g, r, slots, kind):
+        blocks = []
+        for slot in slots:
+            if slot == 0:
+                blocks = [(0, r)] + ([(0, 0)] if r == 1 else []) + blocks
+            elif slot == 8:
+                blocks = [(8, r)] + ([(8, 1)] if r == 0 else []) + blocks
+            else:
+                blocks = blocks + [(slot, 0), (slot, 1)]
+        keys = len(blocks) * HALF
+        mine = pl.ds(r * HALF, HALF)
+
+        def rows_of(ref):
+            return jnp.concatenate([ref[pl.ds(slot * SUPER + half * HALF, HALF), :] for slot, half in blocks], axis=0)
+
+        q = jnp.concatenate(
+            [qbuf[g // 2, mine, (g % 2) * HEAD_SIZE : (g % 2 + 1) * HEAD_SIZE], qdoc[mine, :]], axis=1)
+        k = jnp.concatenate([rows_of(kbuf), rows_of(kdoc)], axis=1)
+        v = jnp.concatenate([rows_of(vbuf), jnp.ones((keys, HEAD_SIZE), jnp.bfloat16)], axis=1)
         s = lax.dot_general(q, k, (((1,), (1,)), ((), ())), preferred_element_type=jnp.float32)
-        if kind != "middle":
-            t = lax.broadcasted_iota(jnp.int32, (SUPER, keys), 0)
-            u = lax.broadcasted_iota(jnp.int32, (SUPER, keys), 1)
-            if kind == "first":
-                s = jnp.where(u <= t, s, NEGATIVE)
-            else:
-                s = jnp.where(u > t + (keys - SUPER), s, NEGATIVE) if slots == 1 else jnp.where(
-                    (u < SUPER) | (u - SUPER > t), s, NEGATIVE)
+        if 0 in slots or 8 in slots:
+            t = lax.broadcasted_iota(jnp.int32, (HALF, HALF), 0)
+            u = lax.broadcasted_iota(jnp.int32, (HALF, HALF), 1)
+            near = jnp.where(u <= t if 0 in slots else u > t, s[:, :HALF], NEGATIVE)
+            s = jnp.concatenate([near, s[:, HALF:]], axis=1)
         high = jnp.max(s, axis=1, keepdims=True)
         if kind != "first":
-            old = top[g][:, :1]
+            old = top[g, mine, :1]
             high = jnp.maximum(high, old)
         p = jnp.exp2(s * SCALE2 - high * SCALE2).astype(jnp.bfloat16)
         part = jnp.dot(p, v, preferred_element_type=jnp.float32)
         if kind != "first":
-            part = part + acc[g] * jnp.exp2((old - high) * SCALE2)
+            part = part + acc[g, mine, :] * jnp.exp2((old - high) * SCALE2)
         if kind == "last":
-            obuf[g // 2, :, (g % 2) * HEAD_SIZE : (g % 2 + 1) * HEAD_SIZE] = (part[:, :HEAD_SIZE] / part[:, HEAD_SIZE:]).astype(jnp.bfloat16)
+            obuf[g // 2, mine, (g % 2) * HEAD_SIZE : (g % 2 + 1) * HEAD_SIZE] = (
+                part[:, :HEAD_SIZE] / part[:, HEAD_SIZE:]).astype(jnp.bfloat16)
         else:
-            acc[g] = part
-            top[g] = jnp.broadcast_to(high, (SUPER, HEAD_SIZE))
-
-    def pair(n, first_slot, slots, kind):
-        for g in (2 * n, 2 * n + 1):
-            attend(g, first_slot, slots, kind)
+            acc[g, mine, :] = part
+            top[g, mine, :] = jnp.broadcast_to(high, (HALF, HEAD_SIZE))
+
+    def pair(n, slots, kind="middle"):
+        def run():
+            for g in (2 * n, 2 * n + 1):
+                for r in (0, 1):
+                    attend(g, r, slots, kind)
+
+        if kind == "middle":
+            pl.when(exists(min(slots)))(run)
+        else:
+            run()
 
     for part in (0, 1):
         loop(8, lambda j: kv_arrive(j, part))
     pass_on(0)
+    pass_on(1)
     whole(0)
-    pass_on(1)
+    whole(2)
     loop(16, lambda i: q_arrive(0, i))
-    pair(0, 0, 1, "first")
+    pair(0, (0, 2), "first")
     loop(16, lambda i: q_arrive(1, i))
-    pair(1, 0, 1, "first")
     pass_on(2)
     pass_odd(0)
-    for i in range(1, 5):
-        whole(2 * i)
-        whole(2 * i - 1)
-        kind = "last" if i == 4 else "middle"
-        pair(0, 2 * i - 1, 2, kind)
-        if i < 3:
-            pass_on(i + 2)
-        if i < 4:
-            pass_odd(i)
-        else:
-            o_send_pair(0)
-        pair(1, 2 * i - 1, 2, kind)
+    pair(1, (0, 2), "first")
+    whole(1)
+    whole(4)
+    pair(0, (1, 4))
+    pass_on(3)
+    pass_odd(1)
+    pair(1, (1, 4))
+    whole(3)
+    whole(6)
+    pair(0, (3, 6))
+    pass_on(4)
+    pass_odd(2)
+    pair(1, (3, 6))
+    whole(8)
+    whole(5)
+    pair(0, (8, 5))
+    pass_odd(3)
+    whole(7)
+    pair(0, (7,), "last")
+    o_send_pair(0)
+    pair(1, (8, 5, 7), "last")
     o_send_pair(1)
 
     for part in (0, 1):
         loop(8, lambda j: kv_copy(j, part, False))
         for d in range(4):
-            z_copy(d, part).wait_send()
-            y_copy(d, part).wait_send()
+            @pl.when(exists(2 * d) & (z < LEVELS - 1))
+            def _():
+                z_copy(d, part).wait_send()
+
+            @pl.when(z >= d + yp)
+            def _():
+                y_copy(d, part).wait_send()
         for slot in range(SLOTS):
-            s_copy(slot, part).wait_send()
+            @pl.when(exists(slot))
+            def _():
+                s_copy(slot, part).wait_send()
     for n in (0, 1):
         loop(16, lambda i: q_copy(n, i, False), 1)
     for n in (0, 1):
@@ -301,6 +378,10 @@
             dma((2, 8)), dma((2, 8)), dma((2, 16)), dma((2, 16)),
             dma((2, 4)), dma((2, 5)), dma((2, 4)), dma((2, 4)),
             dma((2, SLOTS)), dma((2, SLOTS)), dma((2, 16)), dma((2, 16)),
+            pltpu.VMEM((ROWS, QUERY_HEADS * HEAD_SIZE), jnp.bfloat16),
+            pltpu.VMEM((ROWS, KEY_VALUE_HEADS * HEAD_SIZE), jnp.bfloat16),
+            pltpu.VMEM((ROWS, KEY_VALUE_HEADS * HEAD_SIZE), jnp.bfloat16),
+            dma((3,)),
         ],
         compiler_params=pltpu.CompilerParams(
             collective_id=0, has_side_effects=True, vmem_limit_bytes=63 * 2**20),

time: 55.3 us -> 47.6 us (0.86)
  the two profiles are of different devices: /device:TPU:1 before, /device:TPU:193 now
where the time goes in v2:
time: 47.6 us; the launch traced here: 47.3 us
  Pallas kernels  45.4 us (95%)
  local copies, waits for them, and re-layouts  1.87 us (4%)
    pallas_call x1, Pallas kernels, on_device(): pl.pallas_call(kernel, name='packed_attention', out_shape=jax.ShapeDtypeS...  45.4 us
    unnamed x1, local copies, waits for them, and re-layouts  1.87 us

profile of v2, /device:TPU:193, one launch (start us, length us, event | category | flops | bytes accessed | tf_op | source)
XLA Modules:
  0.0 47.3 jit_solution(12087103642506156973)
XLA Ops:
  0.0 45.4 %packed_attention.1 = bf16[32,8192]{1,0:T(8,128)(2,1)} custom-call(bf16[32,8192]{1,0:T(8,128)(2,1)} %q_ref.1, bf16[32,1024]{1,0:T(8,128)(2,1)} %k_ref.1, bf16[32,1024]{1,0:T(8,128)(2,1)} %v_ref.1, s32[16]{0:T(128)} %doc_ref.1), custom_call_target="tpu_custom_call" | custom-call | tf_op jit(solution)/shard_map/packed_attention/pallas_call | solution.py:363
  45.4 1.9 %copy.6 = bf16[32,8192]{1,0:T(8,128)(2,1)} copy(bf16[32,8192]{1,0:T(8,128)(2,1)} %packed_attention.1) | data formatting | bytes 1048576

commit v3 on v2

--- a/solution.py
+++ b/solution.py
@@ -183,10 +183,10 @@
                     y_copy(d - yp, part).start()
                 s_copy(2 * d, part).start()
 
-    def pass_odd(i):
+    def pass_odd(i, parts=(0, 1)):
         @pl.when(exists(2 * i + 1))
         def _():
-            for part in (0, 1):
+            for part in parts:
                 landed(2 * i + 1, core, y_recv.at[part, i], part)
                 s_copy(2 * i + 1, part).start()
 
@@ -220,9 +220,11 @@
 
     for part in (0, 1):
         loop(8, lambda j: kv_copy(j, part, True))
-    for n in (0, 1):
+    def q_send_pair(n):
         q_own(n).start()
         loop(16, lambda i: q_copy(n, i, True), 1)
+
+    q_send_pair(0)
 
     lane = lax.broadcasted_iota(jnp.int32, (1, HEAD_SIZE), 1)
     begins = jnp.where(lane == DOCS, -(1 << 20), 1 << 20)
@@ -264,7 +266,8 @@
         mine = pl.ds(r * HALF, HALF)
 
         def rows_of(ref):
-            return jnp.concatenate([ref[pl.ds(slot * SUPER + half * HALF, HALF), :] for slot, half in blocks], axis=0)
+            parts = [ref[pl.ds(slot * SUPER + half * HALF, HALF), :] for slot, half in blocks]
+            return parts[0] if len(parts) == 1 else jnp.concatenate(parts, axis=0)
 
         q = jnp.concatenate(
             [qbuf[g // 2, mine, (g % 2) * HEAD_SIZE : (g % 2 + 1) * HEAD_SIZE], qdoc[mine, :]], axis=1)
@@ -275,7 +278,7 @@
             t = lax.broadcasted_iota(jnp.int32, (HALF, HALF), 0)
             u = lax.broadcasted_iota(jnp.int32, (HALF, HALF), 1)
             near = jnp.where(u <= t if 0 in slots else u > t, s[:, :HALF], NEGATIVE)
-            s = jnp.concatenate([near, s[:, HALF:]], axis=1)
+            s = near if keys == HALF else jnp.concatenate([near, s[:, HALF:]], axis=1)
         high = jnp.max(s, axis=1, keepdims=True)
         if kind != "first":
             old = top[g, mine, :1]
@@ -302,36 +305,45 @@
         else:
             run()
 
-    for part in (0, 1):
-        loop(8, lambda j: kv_arrive(j, part))
-    pass_on(0)
-    pass_on(1)
+    loop(8, lambda j: kv_arrive(j, 0))
+    pass_on(0, (0,))
+    q_send_pair(1)
+    loop(8, lambda j: kv_arrive(j, 1))
+    pass_on(0, (1,))
+    pass_on(1, (0,))
     whole(0)
+    pass_on(1, (1,))
+    loop(16, lambda i: q_arrive(0, i))
+    pair(0, (0,), "first")
+    pass_on(2, (0,))
     whole(2)
-    loop(16, lambda i: q_arrive(0, i))
-    pair(0, (0, 2), "first")
+    pair(0, (2,))
+    pass_on(2, (1,))
+    pass_on(3, (0,))
+    pass_odd(0)
     loop(16, lambda i: q_arrive(1, i))
-    pass_on(2)
-    pass_odd(0)
     pair(1, (0, 2), "first")
+    pass_on(3, (1,))
+    pass_on(4, (0,))
+    pass_odd(1, (0,))
     whole(1)
     whole(4)
     pair(0, (1, 4))
-    pass_on(3)
-    pass_odd(1)
+    pass_on(4, (1,))
+    pass_odd(1, (1,))
+    pass_odd(2, (0,))
     pair(1, (1, 4))
+    pass_odd(2, (1,))
+    pass_odd(3, (0,))
     whole(3)
     whole(6)
     pair(0, (3, 6))
-    pass_on(4)
-    pass_odd(2)
+    pass_odd(3, (1,))
     pair(1, (3, 6))
     whole(8)
     whole(5)
-    pair(0, (8, 5))
-    pass_odd(3)
     whole(7)
-    pair(0, (7,), "last")
+    pair(0, (8, 5, 7), "last")
     o_send_pair(0)
     pair(1, (8, 5, 7), "last")
     o_send_pair(1)

time: 47.6 us -> 46.8 us (0.983)
  Pallas kernels: 45.4 us -> 44.8 us
    pallas_call x1, Pallas kernels: 45.4 us -> 44.8 us  [on_device(): pl.pallas_call(kernel, name='packed_attention', out_shape=jax.ShapeDtypeS...]
where the time goes in v3:
time: 46.8 us; the launch traced here: 46.7 us
  Pallas kernels  44.8 us (96%)
  local copies, waits for them, and re-layouts  1.87 us (4%)
    pallas_call x1, Pallas kernels, on_device(): pl.pallas_call(kernel, name='packed_attention', out_shape=jax.ShapeDtypeS...  44.8 us
    unnamed x1, local copies, waits for them, and re-layouts  1.87 us

profile of v3, /device:TPU:193, one launch (start us, length us, event | category | flops | bytes accessed | tf_op | source)
XLA Modules:
  0.0 46.7 jit_solution(482278911846982200)
XLA Ops:
  0.0 44.8 %packed_attention.1 = bf16[32,8192]{1,0:T(8,128)(2,1)} custom-call(bf16[32,8192]{1,0:T(8,128)(2,1)} %q_ref.1, bf16[32,1024]{1,0:T(8,128)(2,1)} %k_ref.1, bf16[32,1024]{1,0:T(8,128)(2,1)} %v_ref.1, s32[16]{0:T(128)} %doc_ref.1), custom_call_target="tpu_custom_call" | custom-call | tf_op jit(solution)/shard_map/packed_attention/pallas_call | solution.py:375
  44.8 1.9 %copy.6 = bf16[32,8192]{1,0:T(8,128)(2,1)} copy(bf16[32,8192]{1,0:T(8,128)(2,1)} %packed_attention.1) | data formatting | bytes 1048576

commit v4 on v3

--- a/solution.py
+++ b/solution.py
@@ -67,7 +67,7 @@
 
     pl.semaphore_wait(barrier, 18 - (z == 0).astype(jnp.int32) - (z == LEVELS - 1).astype(jnp.int32))
 
-    for copy in fetch:
+    for copy in fetch[:2]:
         copy.wait()
 
     def remote(src, dst, send, recv, to):
@@ -224,6 +224,7 @@
         q_own(n).start()
         loop(16, lambda i: q_copy(n, i, True), 1)
 
+    fetch[2].wait()
     q_send_pair(0)
 
     lane = lax.broadcasted_iota(jnp.int32, (1, HEAD_SIZE), 1)

time: 46.8 us -> 46.8 us (level)
  no operation moved by 1% of the time
where the time goes in v4:
time: 46.8 us; the launch traced here: 46.7 us
  Pallas kernels  44.8 us (96%)
  local copies, waits for them, and re-layouts  1.87 us (4%)
    pallas_call x1, Pallas kernels, on_device(): pl.pallas_call(kernel, name='packed_attention', out_shape=jax.ShapeDtypeS...  44.8 us
    unnamed x1, local copies, waits for them, and re-layouts  1.87 us

profile of v4, /device:TPU:193, one launch (start us, length us, event | category | flops | bytes accessed | tf_op | source)
XLA Modules:
  0.0 46.7 jit_solution(764922208938949654)
XLA Ops:
  0.0 44.8 %packed_attention.1 = bf16[32,8192]{1,0:T(8,128)(2,1)} custom-call(bf16[32,8192]{1,0:T(8,128)(2,1)} %q_ref.1, bf16[32,1024]{1,0:T(8,128)(2,1)} %k_ref.1, bf16[32,1024]{1,0:T(8,128)(2,1)} %v_ref.1, s32[16]{0:T(128)} %doc_ref.1), custom_call_target="tpu_custom_call" | custom-call | tf_op jit(solution)/shard_map/packed_attention/pallas_call | solution.py:376
  44.8 1.9 %copy.6 = bf16[32,8192]{1,0:T(8,128)(2,1)} copy(bf16[32,8192]{1,0:T(8,128)(2,1)} %packed_attention.1) | data formatting | bytes 1048576
